TPU v7x, 512 devices: a whole 4x4x16 slice. The times are simulated.
512 devices in a mesh: zone: 32 (over z, x_hi), freq: 16 (over x_lo, y, core).
Axes of the slice: x: 4 (x_hi: 2, x_lo: 2; x = x_hi * 2 + x_lo), y: 4, z: 16, core: 2. Of those that a mesh axis runs over, the one named last changes fastest.
Arguments:
- modulus: float32 [256, 3, 1, 1024], P('zone'), may hold values from 0.3 to 1.5
- first_moment: float32 [256, 3, 1, 1024], P('zone'), may hold values from -6 to 6
- second_moment: float32 [256, 3, 1, 1024], P('zone'), may hold values from 0.5 to 4
- fiber: float32 [256, 1, 1024], P('zone'), may hold values from -1 to 1
- measured: float32 [16, 128, 2, 8, 1024], P('freq', 'zone'), may hold values from -6 to 6
- wave_sq: float32 [16], P('freq'), may hold values from 0.5 to 5
- send_list: int32 [32, 32, 2], P('zone'), may hold values from -1 to 7, as said below
- brick_list: int32 [128, 8], P('zone'), may hold values from 0 to 63, as said below
Outputs:
- new_modulus: float32 [256, 3, 1, 1024], P('zone')
- new_first: float32 [256, 3, 1, 1024], P('zone')
- new_second: float32 [256, 3, 1, 1024], P('zone')
Inputs may be any that keep to these rules, and one draw needn't show every extreme that they name: `send_list`: entries are -1 or distinct local brick indices; for each owner and zone group the live slots are c < some count of 0 to 2, and owner o sends 2 bricks to group (o + 1) % 32. `brick_list`: every entry names a live slot of its zone group.
All inputs are finite; a program needn't handle non-finite values.
Results may differ from a plain program's by a relative error of at most 0.0001.
Values sent between devices are 32-bit elements; how exact they have to be, the bound alone decides.
A program may use at most 64 MiB of HBM per device.

v0:
```python
import jax
import jax.numpy as jnp
from jax import lax
from jax.sharding import PartitionSpec as P

BY = 32
BZ = 32
K = 8
SWEEPS = 6
relax_rate = 0.25
learn_rate = 0.1
beta_first = 0.9
beta_second = 0.99
smooth_rate = 0.5
adam_eps = 1e-08


def beside_sum(cube):
    padded = jnp.pad(cube, ((0, 0), (1, 1), (1, 1), (1, 1)))
    total = padded[:, 2:, 1:-1, 1:-1] + padded[:, :-2, 1:-1, 1:-1]
    total = total + padded[:, 1:-1, 2:, 1:-1] + padded[:, 1:-1, :-2, 1:-1]
    return total + padded[:, 1:-1, 1:-1, 2:] + padded[:, 1:-1, 1:-1, :-2]


def misfit(moduli, fiber_tile, observed, wave_value):
    shear = (moduli[0] + (moduli[1] - moduli[0]) * fiber_tile * fiber_tile).reshape(-1, BY, BZ)
    damping = moduli[2].reshape(-1, BY, BZ)
    diagonal_term = 6.0 * shear + wave_value
    start_field = observed.reshape(2, -1, BY, BZ)
    field = start_field
    for sweep_index in range(SWEEPS):
        stencil = 6.0 * field - beside_sum(field)
        resid_real = shear * (stencil[0] - damping * stencil[1]) - wave_value * field[0]
        resid_imag = shear * (stencil[1] + damping * stencil[0]) - wave_value * field[1]
        field = field - relax_rate * jnp.stack([resid_real, resid_imag]) / diagonal_term
    gap = field - start_field
    return jnp.sum(gap * gap)


def update(moduli, first_moment, second_moment, fiber_tile, descent):
    new_first = beta_first * first_moment + (1.0 - beta_first) * descent
    new_second = beta_second * second_moment + (1.0 - beta_second) * descent * descent
    stepped = moduli - learn_rate * new_first / (jnp.sqrt(new_second) + adam_eps)
    shaped = stepped.reshape(stepped.shape[:-1] + (-1, BZ))
    lower_cell = jnp.concatenate([shaped[..., :1], shaped[..., :-1]], axis=-1).reshape(
        stepped.shape
    )
    upper_cell = jnp.concatenate([shaped[..., 1:], shaped[..., -1:]], axis=-1).reshape(
        stepped.shape
    )
    weight = smooth_rate * (fiber_tile * fiber_tile)[:, None]
    smoothed = stepped + weight * (0.5 * (lower_cell + upper_cell) - stepped)
    return (smoothed, new_first, new_second)


def to_owned(returned, owner_pick):
    flattened = returned.reshape(owner_pick.shape[1], -1)
    return jnp.dot(owner_pick, flattened, precision=lax.Precision.HIGHEST)


def on_device(
    modulus, first_moment, second_moment, fiber, measured, wave_sq, send_list, brick_list
):
    zone_count = lax.axis_size("zone")
    freq_count = lax.axis_size("freq")
    owned_count = modulus.shape[0]
    rows_brick = modulus.shape[2]
    depth = modulus.shape[3]
    slot_cap = send_list.shape[2]
    owner_list = send_list[0]
    live_mask = owner_list >= 0
    safe_ids = jnp.where(live_mask, owner_list, 0)
    stacked = jnp.concatenate([modulus, fiber[:, None]], axis=1)
    outgoing = jnp.where(live_mask[:, :, None, None, None], stacked[safe_ids], 0.0)
    arrived = lax.all_to_all(outgoing, "zone", split_axis=0, concat_axis=0, tiled=True)
    slot_data = arrived.reshape(zone_count * slot_cap, 4, rows_brick, depth)
    wave_value = wave_sq[0]

    def solve(subzone_item):
        brick_ids, observed = subzone_item
        picked_rows = slot_data[brick_ids]
        subzone_par = jnp.swapaxes(picked_rows, 0, 1).reshape(4, K * rows_brick, depth)
        gradient = jax.grad(misfit)(subzone_par[:3], subzone_par[3], observed, wave_value)
        return jnp.swapaxes(gradient.reshape(3, K, rows_brick, depth), 0, 1)

    gradients = lax.map(solve, (brick_list, measured[0]))
    flattened = gradients.reshape(-1, 3 * rows_brick * depth)
    references = brick_list.reshape(-1)
    slot_iota = jnp.arange(zone_count * slot_cap, dtype=jnp.int32)
    selector = (references[None, :] == slot_iota[:, None]).astype(jnp.float32)
    slot_grad = jnp.dot(selector, flattened, precision=lax.Precision.HIGHEST)
    slot_grad = slot_grad.reshape(zone_count, slot_cap, 3, rows_brick, depth)
    use_count = jnp.sum(selector, axis=1).reshape(zone_count, slot_cap)
    owned_iota = jnp.arange(owned_count, dtype=jnp.int32)
    owner_pick = (owner_list.reshape(-1)[None, :] == owned_iota[:, None]).astype(jnp.float32)
    returned, returned_uses = (
        lax.all_to_all(slot_grad, "zone", split_axis=0, concat_axis=0, tiled=True),
        lax.all_to_all(use_count, "zone", split_axis=0, concat_axis=0, tiled=True),
    )
    owned_grad = to_owned(returned, owner_pick).reshape(owned_count, 3, rows_brick, depth)
    intersection = jnp.dot(owner_pick, returned_uses.reshape(-1), precision=lax.Precision.HIGHEST)
    grad_total = lax.psum(owned_grad, "freq")
    descent = grad_total / (freq_count * jnp.maximum(intersection, 1.0))[:, None, None, None]
    return update(modulus, first_moment, second_moment, fiber, descent)


def solution(mesh):
    placed = (
        P("zone", None, None, None),
        P("zone", None, None, None),
        P("zone", None, None, None),
        P("zone", None, None),
        P("freq", "zone", None, None, None),
        P("freq"),
        P("zone", None, None),
        P("zone", None),
    )
    return jax.shard_map(
        on_device,
        mesh=mesh,
        in_specs=placed,
        out_specs=(
            P("zone", None, None, None),
            P("zone", None, None, None),
            P("zone", None, None, None),
        ),
        check_vma=False,
    )
```

profile of v0, /device:TPU:1, one launch (start us, length us, event | category | flops | bytes accessed | tf_op | source)
XLA Modules:
  0.0 472.6 jit_solution(13486487006673301540)
XLA Ops:
  8.3 1.0 pad_maximum_fusion
  9.3 1.2 gather_fusion.1
  10.5 1.3 broadcast_select_fusion
  11.8 18.5 %all-to-all-start = ((f32[32,2,4,1,1024]{4,2,1,3,0:T(4,128)}), f32[32,2,4,1,1024]{4,2,1,3,0:T(4,128)S(1)}, u32[]{:S(2)}, u32[]{:S(2)}) async-start(f32[32,2,4,1,1024]{4,2,1,3,0:T(4,128)} %broadcast_select_fusion), calls=%async_computation | async-start | bytes 2097152 | tf_op jit(solution)/shard_map/all_to_all | solution.py:75
  32.9 50.5 %all-to-all-done = f32[32,2,4,1,1024]{4,2,1,3,0:T(4,128)S(1)} async-done(((f32[32,2,4,1,1024]{4,2,1,3,0:T(4,128)}), f32[32,2,4,1,1024]{4,2,1,3,0:T(4,128)S(1)}, u32[]{:S(2)}, u32[]{:S(2)}) %all-to-all-start) | async-done | bytes 1048608 | tf_op jit(solution)/shard_map/all_to_all | solution.py:75
  83.4 7.2 %all-to-all-start.2 = ((f32[32,1,2]{2,1,0:T(1,128)}), f32[32,1,2]{2,1,0:T(1,128)S(1)}, u32[]{:S(2)}, u32[]{:S(2)}) async-start(f32[32,1,2]{2,1,0:T(1,128)} %bitcast.32), calls=%async_computation.2 | async-start | bytes 32768 | tf_op jit(solution)/shard_map/all_to_all | solution.py:98
  90.6 189.0 %while.12 = (s32[]{:T(128)}, f32[4,8,3,1,1024]{4,1,2,3,0:T(8,128)}, s32[4,8]{1,0:T(4,128)}, f32[64,4,1,1024]{3,1,0,2:T(4,128)S(1)}, f32[4,2,8,1024]{3,2,1,0:T(8,...) while((s32[]{:T(128)}, f32[4,8,3,1,1024]{4,1,2,3,0:T(8,128)}, s32[4,8]{1,0:T(4,128)}, ...), condition=%wide.region_7.8_spmd, body=%wide.region_0.7_spmd.sunk | while | flops 7111707 | bytes 32707772 | solution.py:86
  91.4 1.4 dynamic-slice_multiply_fusion.3
  96.0 1.4 multiply_divide_fusion.4
  113.3 0.9 multiply_reduce_fusion.9
  123.0 1.4 fusion.211
  126.0 0.9 copy-done.5
  127.1 1.5 fusion.213
  128.6 1.6 unstack.190
  131.0 0.9 copy-done.3
  131.9 1.0 divide_multiply_fusion.17
  138.6 1.4 dynamic-slice_multiply_fusion.3
  143.2 1.4 multiply_divide_fusion.4
  160.5 0.9 multiply_reduce_fusion.9
  170.3 1.4 fusion.211
  173.2 0.9 copy-done.5
  174.4 1.5 fusion.213
  175.8 1.6 unstack.190
  178.2 0.9 copy-done.3
  179.1 1.0 divide_multiply_fusion.17
  185.8 1.4 dynamic-slice_multiply_fusion.3
  190.5 1.4 multiply_divide_fusion.4
  207.8 0.9 multiply_reduce_fusion.9
  217.5 1.4 fusion.211
  220.4 0.9 copy-done.5
  221.6 1.5 fusion.213
  223.1 1.6 unstack.190
  226.4 1.0 divide_multiply_fusion.17
  233.1 1.4 dynamic-slice_multiply_fusion.3
  237.7 1.4 multiply_divide_fusion.4
  255.0 0.9 multiply_reduce_fusion.9
  264.7 1.4 fusion.211
  267.7 0.9 copy-done.5
  268.8 1.5 fusion.213
  270.3 1.6 unstack.190
  273.6 1.0 divide_multiply_fusion.17
  280.3 1.5 convolution_bitcast_fusion
  281.8 1.5 copy.104
  283.3 14.0 %all-to-all-start.1 = ((f32[32,2,3,1,1024]{4,1,3,2,0:T(2,128)}), f32[32,2,3,1,1024]{4,1,3,2,0:T(2,128)S(1)}, u32[]{:S(2)}, u32[]{:S(2)}) async-start(f32[32,2,3,1,1024]{4,1,3,2,0:T(2,128)} %copy.104), calls=%async_computation.1 | async-start | bytes 1572864 | tf_op jit(solution)/shard_map/all_to_all | solution.py:97
  299.4 39.1 %all-to-all-done.1 = f32[32,2,3,1,1024]{4,1,3,2,0:T(2,128)S(1)} async-done(((f32[32,2,3,1,1024]{4,1,3,2,0:T(2,128)}), f32[32,2,3,1,1024]{4,1,3,2,0:T(2,128)S(1)}, u32[]{:S(2)}, u32[]{:S(2)}) %all-to-all-start.1) | async-done | bytes 786464 | tf_op jit(solution)/shard_map/all_to_all | solution.py:97
  339.0 1.5 convolution_bitcast_fusion.1
  340.6 120.9 %all-reduce.72.cloned.1.call-done = f32[8,3,1,1024]{3,0,1,2:T(8,128)} async-done(((f32[8,3,1,1024]{3,0,1,2:T(8,128)}), f32[8,3,1,1024]{3,0,1,2:T(8,128)}) %all-reduce.72.cloned.1.call-update) | async-done | bytes 98320 | tf_op jit(solution)/shard_map/psum | solution.py:102
  461.5 1.0 copy_subtract_fusion
  (711 shorter events, 155.0 us)
Async XLA Ops:
  7.2 1.1 copy-start.33
  11.8 71.6 %all-to-all-start = ((f32[32,2,4,1,1024]{4,2,1,3,0:T(4,128)}), f32[32,2,4,1,1024]{4,2,1,3,0:T(4,128)S(1)}, u32[]{:S(2)}, u32[]{:S(2)}) async-start(f32[32,2,4,1,1024]{4,2,1,3,0:T(4,128)} %broadcast_select_fusion), calls=%async_computation | async-start | bytes 2097152 | tf_op jit(solution)/shard_map/all_to_all | solution.py:75
  83.4 199.9 %all-to-all-start.2 = ((f32[32,1,2]{2,1,0:T(1,128)}), f32[32,1,2]{2,1,0:T(1,128)S(1)}, u32[]{:S(2)}, u32[]{:S(2)}) async-start(f32[32,1,2]{2,1,0:T(1,128)} %bitcast.32), calls=%async_computation.2 | async-start | bytes 32768 | tf_op jit(solution)/shard_map/all_to_all | solution.py:98
  90.6 4.7 copy-start.30
  94.6 1.1 copy-start.1
  125.9 0.9 copy-start.5
  130.9 0.9 copy-start.3
  130.9 1.0 copy-start.4
  131.9 1.0 copy-start.6
  133.7 1.0 copy-start
  134.9 0.9 copy-start.15
  134.9 0.9 copy-start.16
  136.6 1.3 copy-start.31
  137.9 4.7 copy-start.30
  141.9 1.1 copy-start.1
  173.1 0.9 copy-start.5
  178.2 0.9 copy-start.3
  178.2 1.0 copy-start.4
  179.1 1.0 copy-start.6
  181.0 1.0 copy-start
  182.1 0.9 copy-start.15
  182.1 0.9 copy-start.16
  183.9 1.3 copy-start.31
  185.1 4.7 copy-start.30
  189.1 1.1 copy-start.1
  220.4 0.9 copy-start.5
  225.4 0.9 copy-start.3
  225.4 1.0 copy-start.4
  226.4 1.0 copy-start.6
  228.2 1.0 copy-start
  229.3 0.9 copy-start.15
  229.3 0.9 copy-start.16
  231.1 1.3 copy-start.31
  232.4 4.7 copy-start.30
  236.3 1.1 copy-start.1
  267.6 0.9 copy-start.5
  272.6 0.9 copy-start.3
  272.6 1.0 copy-start.4
  273.6 1.0 copy-start.6
  275.4 1.0 copy-start
  276.6 0.9 copy-start.16
  278.3 1.3 copy-start.31
  283.3 14.1 %copy-start.38 = (s32[1,32,2]{1,2,0:T(2,128)S(1)}, s32[1,32,2]{1,2,0:T(2,128)}, u32[]{:S(2)}) copy-start(s32[1,32,2]{1,2,0:T(2,128)} %param.16) | copy-start | bytes 772
  283.3 55.2 %all-to-all-start.1 = ((f32[32,2,3,1,1024]{4,1,3,2,0:T(2,128)}), f32[32,2,3,1,1024]{4,1,3,2,0:T(2,128)S(1)}, u32[]{:S(2)}, u32[]{:S(2)}) async-start(f32[32,2,3,1,1024]{4,1,3,2,0:T(2,128)} %copy.104), calls=%async_computation.1 | async-start | bytes 1572864 | tf_op jit(solution)/shard_map/all_to_all | solution.py:97
  297.3 164.2 %all-reduce.72.cloned.1.call-start = ((), (), s32[]{:S(2)}) async-start(), calls=%async_computation.3 | async-start | bytes 196608 | tf_op jit(solution)/shard_map/psum | solution.py:102
  339.0 122.5 %copy-start.35 = (f32[8,3,1,1024]{3,2,1,0:T(1,128)S(1)}, f32[8,3,1,1024]{3,2,1,0:T(1,128)}, u32[]{:S(2)}) copy-start(f32[8,3,1,1024]{3,2,1,0:T(1,128)} %param.11) | copy-start | bytes 294916
  339.0 122.5 %copy-start.36 = (f32[8,3,1,1024]{3,2,1,0:T(1,128)S(1)}, f32[8,3,1,1024]{3,2,1,0:T(1,128)}, u32[]{:S(2)}) copy-start(f32[8,3,1,1024]{3,2,1,0:T(1,128)} %param.12) | copy-start | bytes 294916
  340.5 121.1 %copy-start.32 = (f32[8,3,1,1024]{3,2,1,0:T(1,128)S(1)}, f32[8,3,1,1024]{3,2,1,0:T(1,128)}, u32[]{:S(2)}) copy-start(f32[8,3,1,1024]{3,2,1,0:T(1,128)} %param.10) | copy-start | bytes 294916
  (94 other events, 77.4 us)
Sparse Core Ops, SparseCore 0:
  340.6 120.8 all-reduce.71
where the time goes:
time: 476 us; the launch traced here: 473 us
  waiting for transfers between devices  211 us (44%)
  local copies, waits for them, and re-layouts  114 us (24%)
  other arithmetic  89.2 us (19%)
  starting transfers between devices  39.7 us (8%)
  between operations  14.2 us (3%)
    psum x1, waiting for transfers between devices, on_device(): grad_total = lax.psum(owned_grad, 'freq')  121 us
    all_to_all x1, waiting for transfers between devices, on_device(): lax.all_to_all(outgoing, 'zone', split_axis=0, concat_axis=0, tiled=True)  50.5 us
    all_to_all x1, waiting for transfers between devices, on_device(): lax.all_to_all(slot_grad, 'zone', split_axis=0, concat_axis=0, tiled=True)  39.1 us
    another operation x100, local copies, waits for them, and re-layouts, misfit(): jnp.stack([resid_real, resid_imag])  38.8 us
    another operation x20, other arithmetic, misfit(): jnp.stack([resid_real, resid_imag])  20.5 us
    all_to_all x1, starting transfers between devices, on_device(): lax.all_to_all(outgoing, 'zone', split_axis=0, concat_axis=0, tiled=True)  18.5 us
    squeeze x24, local copies, waits for them, and re-layouts, misfit(): stencil[0] - damping * stencil[1]  17.5 us
    squeeze x24, local copies, waits for them, and re-layouts, misfit(): stencil[1]  17.4 us
  transfers between devices with their start and end apart: 4, of which 3 were waited for; matrix products, arithmetic and copies ran while one was open for 38% of the time, Pallas kernels for 0%

commit v1 on v0

--- a/solution.py
+++ b/solution.py
@@ -1,3 +1,4 @@
+import functools
 import jax
 import jax.numpy as jnp
 from jax import lax
@@ -13,6 +14,13 @@
 beta_second = 0.99
 smooth_rate = 0.5
 adam_eps = 1e-08
+
+
+def _expand_things(sample, row_axis):
+    return lax.all_gather(sample, row_axis).sum(axis=0)
+
+
+fit_routes_all = functools.partial(_expand_things, row_axis="freq")
 
 
 def beside_sum(cube):
@@ -99,7 +107,7 @@
     )
     owned_grad = to_owned(returned, owner_pick).reshape(owned_count, 3, rows_brick, depth)
     intersection = jnp.dot(owner_pick, returned_uses.reshape(-1), precision=lax.Precision.HIGHEST)
-    grad_total = lax.psum(owned_grad, "freq")
+    grad_total = fit_routes_all(owned_grad)
     descent = grad_total / (freq_count * jnp.maximum(intersection, 1.0))[:, None, None, None]
     return update(modulus, first_moment, second_moment, fiber, descent)
 

time: 476 us -> 373 us (0.78)
  waiting for transfers between devices: 211 us -> 120 us
  local copies, waits for them, and re-layouts: 114 us -> 102 us
  starting transfers between devices: 39.7 us -> 33.4 us
  other arithmetic: 89.2 us -> 94.9 us
    psum x1 -> x0, waiting for transfers between devices: 121 us -> none  [on_device(): grad_total = lax.psum(owned_grad, 'freq')]
    all_to_all x1, waiting for transfers between devices: 0.01 us -> 13.4 us  [on_device(): lax.all_to_all(use_count, 'zone', split_axis=0, concat_axis=0, tiled=True)]
    while x260 -> x220, local copies, waits for them, and re-layouts: 13.7 us -> 0.51 us
    all_gather x0 -> x1, waiting for transfers between devices: none -> 12.5 us  [_expand_things(): return lax.all_gather(sample, row_axis).sum(axis=0)]
    mul x24, other arithmetic: 10.8 us -> 18.3 us  [misfit(): relax_rate * jnp.stack([resid_real, resid_imag]) / diagonal_term]
    all_to_all x1, starting transfers between devices: 14 us -> 7.01 us  [on_device(): lax.all_to_all(slot_grad, 'zone', split_axis=0, concat_axis=0, tiled=True)]
    gather x4, local copies, waits for them, and re-layouts: 2.5 us -> 7.4 us  [solve(): picked_rows = slot_data[brick_ids]]
  transfers between devices with their start and end apart: 4 -> 4, of which waited for: 3 -> 4; matrix products, arithmetic and copies ran while one was open for 38% -> 0% of each run, Pallas kernels for 0% -> 0%
where the time goes in v1:
time: 373 us; the launch traced here: 371 us
  waiting for transfers between devices  120 us (32%)
  local copies, waits for them, and re-layouts  102 us (27%)
  other arithmetic  94.9 us (25%)
  starting transfers between devices  33.4 us (9%)
  between operations  14.3 us (4%)
    all_to_all x1, waiting for transfers between devices, on_device(): lax.all_to_all(outgoing, 'zone', split_axis=0, concat_axis=0, tiled=True)  53 us
    all_to_all x1, waiting for transfers between devices, on_device(): lax.all_to_all(slot_grad, 'zone', split_axis=0, concat_axis=0, tiled=True)  41.2 us
    another operation x100, local copies, waits for them, and re-layouts, misfit(): jnp.stack([resid_real, resid_imag])  38.6 us
    another operation x20, other arithmetic, misfit(): jnp.stack([resid_real, resid_imag])  20.6 us
    all_to_all x1, starting transfers between devices, on_device(): lax.all_to_all(outgoing, 'zone', split_axis=0, concat_axis=0, tiled=True)  18.8 us
    mul x24, other arithmetic, misfit(): relax_rate * jnp.stack([resid_real, resid_imag]) / diagonal_term  18.3 us
    squeeze x24, local copies, waits for them, and re-layouts, misfit(): stencil[0] - damping * stencil[1]  17.4 us
    squeeze x24, local copies, waits for them, and re-layouts, misfit(): stencil[1]  17.3 us
  transfers between devices with their start and end apart: 4, of which 4 were waited for; matrix products, arithmetic and copies ran while one was open for 0% of the time, Pallas kernels for 0%

profile of v1, /device:TPU:1, one launch (start us, length us, event | category | flops | bytes accessed | tf_op | source)
XLA Modules:
  0.0 371.3 jit_solution(4326747618494390581)
XLA Ops:
  8.8 1.0 pad_maximum_fusion
  9.9 1.2 gather_fusion.1
  11.1 1.3 broadcast_select_fusion
  12.4 18.8 %all-to-all-start = ((f32[32,2,4,1,1024]{4,2,1,3,0:T(4,128)}), f32[32,2,4,1,1024]{4,2,1,3,0:T(4,128)}, u32[]{:S(2)}, u32[]{:S(2)}) async-start(f32[32,2,4,1,1024]{4,2,1,3,0:T(4,128)} %broadcast_select_fusion), calls=%async_computation | async-start | bytes 2097152 | tf_op jit(solution)/shard_map/all_to_all | solution.py:83
  31.2 53.0 %all-to-all-done = f32[32,2,4,1,1024]{4,2,1,3,0:T(4,128)} async-done(((f32[32,2,4,1,1024]{4,2,1,3,0:T(4,128)}), f32[32,2,4,1,1024]{4,2,1,3,0:T(4,128)}, u32[]{:S(2)}, u32[]{:S(2)}) %all-to-all-start) | async-done | bytes 1048608 | tf_op jit(solution)/shard_map/all_to_all | solution.py:83
  84.2 186.0 %while.12 = (s32[]{:T(128)}, f32[4,8,3,1,1024]{4,1,2,3,0:T(8,128)}, s32[4,8]{1,0:T(4,128)S(1)}, f32[64,4,1,1024]{3,1,0,2:T(4,128)}, f32[4,2,8,1024]{3,2,1,0:T(8,...) while((s32[]{:T(128)}, f32[4,8,3,1,1024]{4,1,2,3,0:T(8,128)}, s32[4,8]{1,0:T(4,128)S(1)}, ...), condition=%wide.region_7.8_spmd, body=%wide.region_0.7_spmd.sunk | while | flops 7111707 | bytes 23925808 | solution.py:94
  84.2 1.4 dynamic-slice_multiply_fusion.3
  86.6 1.8 gather_fusion
  90.1 1.3 multiply_divide_fusion.4
  107.3 0.9 multiply_reduce_fusion.9
  117.0 1.4 fusion.212
  119.9 1.2 divide_multiply_fusion.16
  121.1 1.5 fusion.214
  122.6 1.7 unstack.190
  125.0 2.0 divide_multiply_fusion.17
  130.7 1.4 dynamic-slice_multiply_fusion.3
  133.1 1.8 gather_fusion
  136.6 1.3 multiply_divide_fusion.4
  163.5 1.4 fusion.212
  166.4 1.2 divide_multiply_fusion.16
  167.6 1.5 fusion.214
  169.1 1.7 unstack.190
  171.5 2.0 divide_multiply_fusion.17
  177.2 1.4 dynamic-slice_multiply_fusion.3
  179.6 1.8 gather_fusion
  183.1 1.3 multiply_divide_fusion.4
  210.0 1.4 fusion.212
  212.9 1.2 divide_multiply_fusion.16
  214.1 1.5 fusion.214
  215.6 1.7 unstack.190
  218.0 2.0 divide_multiply_fusion.17
  223.7 1.4 dynamic-slice_multiply_fusion.3
  226.1 1.8 gather_fusion
  229.6 1.3 multiply_divide_fusion.4
  256.5 1.4 fusion.212
  259.4 1.2 divide_multiply_fusion.16
  260.6 1.5 fusion.214
  262.1 1.7 unstack.190
  264.5 2.0 divide_multiply_fusion.17
  270.2 1.5 convolution_bitcast_fusion
  271.7 1.5 copy.98
  273.2 7.0 %all-to-all-start.1 = ((f32[32,2,3,1,1024]{4,1,3,2,0:T(2,128)}), f32[32,2,3,1,1024]{4,1,3,2,0:T(2,128)S(1)}, u32[]{:S(2)}, u32[]{:S(2)}) async-start(f32[32,2,3,1,1024]{4,1,3,2,0:T(2,128)} %copy.98), calls=%async_computation.1 | async-start | bytes 1572864 | tf_op jit(solution)/shard_map/all_to_all | solution.py:105
  280.5 41.2 %all-to-all-done.1 = f32[32,2,3,1,1024]{4,1,3,2,0:T(2,128)S(1)} async-done(((f32[32,2,3,1,1024]{4,1,3,2,0:T(2,128)}), f32[32,2,3,1,1024]{4,1,3,2,0:T(2,128)S(1)}, u32[]{:S(2)}, u32[]{:S(2)}) %all-to-all-start.1) | async-done | bytes 786464 | tf_op jit(solution)/shard_map/all_to_all | solution.py:105
  322.2 1.5 fusion.126
  324.4 7.6 %all-to-all-start.2 = ((f32[32,1,2]{2,1,0:T(1,128)}), f32[32,1,2]{2,1,0:T(1,128)S(1)}, u32[]{:S(2)}, u32[]{:S(2)}) async-start(f32[32,1,2]{2,1,0:T(1,128)} %bitcast.34), calls=%async_computation.2 | async-start | bytes 32768 | tf_op jit(solution)/shard_map/all_to_all | solution.py:106
  332.1 13.4 %all-to-all-done.2 = f32[32,1,2]{2,1,0:T(1,128)S(1)} async-done(((f32[32,1,2]{2,1,0:T(1,128)}), f32[32,1,2]{2,1,0:T(1,128)S(1)}, u32[]{:S(2)}, u32[]{:S(2)}) %all-to-all-start.2) | async-done | bytes 288 | tf_op jit(solution)/shard_map/all_to_all | solution.py:106
  347.0 12.5 %all-gather.3.cloned.1.call-done = f32[128,3,1024]{2,0,1:T(8,128)} async-done(((f32[8,3,1024]{2,0,1:T(8,128)}), f32[128,3,1024]{2,0,1:T(8,128)}) %all-gather.3.cloned.1.call-update) | async-done | bytes 1572880 | tf_op jit(solution)/shard_map/all_gather | solution.py:20
  359.5 1.5 bitcast_reduce_fusion
  (664 shorter events, 140.6 us)
Async XLA Ops:
  12.4 18.8 %copy-start.32 = (s32[4,8]{1,0:T(4,128)S(1)}, s32[4,8]{1,0:T(4,128)}, u32[]{:S(2)}) copy-start(s32[4,8]{1,0:T(4,128)} %param.17) | copy-start | bytes 388
  12.4 71.9 %all-to-all-start = ((f32[32,2,4,1,1024]{4,2,1,3,0:T(4,128)}), f32[32,2,4,1,1024]{4,2,1,3,0:T(4,128)}, u32[]{:S(2)}, u32[]{:S(2)}) async-start(f32[32,2,4,1,1024]{4,2,1,3,0:T(4,128)} %broadcast_select_fusion), calls=%async_computation | async-start | bytes 2097152 | tf_op jit(solution)/shard_map/all_to_all | solution.py:83
  88.7 1.3 copy-start.1
  122.6 4.4 %copy-start.3 = (f32[8,32,32]{2,1,0:T(8,128)S(1)}, f32[8,32,32]{2,1,0:T(8,128)}, u32[]{:S(2)}) copy-start(f32[8,32,32]{2,1,0:T(8,128)} %get-tuple-element.399) | copy-start | bytes 98308 | tf_op jit(solution)/shard_map/while
  127.4 1.2 copy-start.4
  127.4 1.2 copy-start.5
  127.4 1.2 copy-start.6
  127.4 1.2 copy-start.7
  127.4 1.2 copy-start.8
  127.4 1.2 copy-start.9
  127.5 1.2 copy-start.10
  127.5 1.2 copy-start.11
  127.5 1.2 copy-start.12
  127.5 1.2 copy-start.13
  127.5 1.2 copy-start.14
  127.5 1.2 copy-start.15
  127.5 1.2 copy-start.16
  127.5 1.2 copy-start.17
  127.5 1.2 copy-start.18
  127.5 1.2 copy-start.19
  127.6 1.2 copy-start.20
  127.6 1.2 copy-start.21
  127.6 1.2 copy-start.22
  127.6 1.2 copy-start.23
  127.9 1.5 copy-start.2
  135.2 1.3 copy-start.1
  169.1 4.4 %copy-start.3 = (f32[8,32,32]{2,1,0:T(8,128)S(1)}, f32[8,32,32]{2,1,0:T(8,128)}, u32[]{:S(2)}) copy-start(f32[8,32,32]{2,1,0:T(8,128)} %get-tuple-element.399) | copy-start | bytes 98308 | tf_op jit(solution)/shard_map/while
  173.9 1.2 copy-start.4
  173.9 1.2 copy-start.5
  174.4 1.5 copy-start.2
  181.7 1.3 copy-start.1
  215.6 4.4 %copy-start.3 = (f32[8,32,32]{2,1,0:T(8,128)S(1)}, f32[8,32,32]{2,1,0:T(8,128)}, u32[]{:S(2)}) copy-start(f32[8,32,32]{2,1,0:T(8,128)} %get-tuple-element.399) | copy-start | bytes 98308 | tf_op jit(solution)/shard_map/while
  220.4 1.2 copy-start.4
  220.4 1.2 copy-start.5
  220.9 1.5 copy-start.2
  228.2 1.3 copy-start.1
  262.1 4.4 %copy-start.3 = (f32[8,32,32]{2,1,0:T(8,128)S(1)}, f32[8,32,32]{2,1,0:T(8,128)}, u32[]{:S(2)}) copy-start(f32[8,32,32]{2,1,0:T(8,128)} %get-tuple-element.399) | copy-start | bytes 98308 | tf_op jit(solution)/shard_map/while
  266.9 1.2 copy-start.4
  266.9 1.2 copy-start.5
  267.4 1.5 copy-start.2
  271.7 8.6 %copy-start.31 = (s32[1,32,2]{1,2,0:T(2,128)S(1)}, s32[1,32,2]{1,2,0:T(2,128)}, u32[]{:S(2)}) copy-start(s32[1,32,2]{1,2,0:T(2,128)} %param.16) | copy-start | bytes 772
  273.2 48.5 %all-to-all-start.1 = ((f32[32,2,3,1,1024]{4,1,3,2,0:T(2,128)}), f32[32,2,3,1,1024]{4,1,3,2,0:T(2,128)S(1)}, u32[]{:S(2)}, u32[]{:S(2)}) async-start(f32[32,2,3,1,1024]{4,1,3,2,0:T(2,128)} %copy.98), calls=%async_computation.1 | async-start | bytes 1572864 | tf_op jit(solution)/shard_map/all_to_all | solution.py:105
  280.2 51.8 %copy-start.28 = (f32[8,1,1024]{2,1,0:T(1,128)S(1)}, f32[8,1,1024]{2,1,0:T(1,128)}, u32[]{:S(2)}) copy-start(f32[8,1,1024]{2,1,0:T(1,128)} %param.13) | copy-start | bytes 98308
  280.2 79.3 %all-gather.3.cloned.1.call-start = ((), (), s32[]{:S(2)}) async-start(), calls=%async_computation.3 | async-start | bytes 1671168 | tf_op jit(solution)/shard_map/all_gather | solution.py:20
  322.1 38.9 %copy-start.27 = (f32[8,3,1,1024]{3,2,1,0:T(1,128)S(1)}, f32[8,3,1,1024]{3,2,1,0:T(1,128)}, u32[]{:S(2)}) copy-start(f32[8,3,1,1024]{3,2,1,0:T(1,128)} %param.10) | copy-start | bytes 294916
  322.1 38.9 %copy-start.29 = (f32[8,3,1,1024]{3,2,1,0:T(1,128)S(1)}, f32[8,3,1,1024]{3,2,1,0:T(1,128)}, u32[]{:S(2)}) copy-start(f32[8,3,1,1024]{3,2,1,0:T(1,128)} %param.11) | copy-start | bytes 294916
  322.1 38.9 %copy-start.30 = (f32[8,3,1,1024]{3,2,1,0:T(1,128)S(1)}, f32[8,3,1,1024]{3,2,1,0:T(1,128)}, u32[]{:S(2)}) copy-start(f32[8,3,1,1024]{3,2,1,0:T(1,128)} %param.12) | copy-start | bytes 294916
  324.4 21.1 %all-to-all-start.2 = ((f32[32,1,2]{2,1,0:T(1,128)}), f32[32,1,2]{2,1,0:T(1,128)S(1)}, u32[]{:S(2)}, u32[]{:S(2)}) async-start(f32[32,1,2]{2,1,0:T(1,128)} %bitcast.34), calls=%async_computation.2 | async-start | bytes 32768 | tf_op jit(solution)/shard_map/all_to_all | solution.py:106
  (70 other events, 85.2 us)
Sparse Core Ops, SparseCore 0:
  323.8 35.7 all-gather.2
